TPU v7x, 256 devices: a whole 4x4x8 slice. The times are simulated.
256 devices in a mesh: lat: 8 (over x_lo, y), lon: 32 (over x_hi, z, core).
Axes of the slice: x: 4 (x_hi: 2, x_lo: 2; x = x_hi * 2 + x_lo), y: 4, z: 8, core: 2. Of those that a mesh axis runs over, the one named last changes fastest.
Arguments:
- field: bfloat16 [2, 144, 768, 512], P(None, 'lat', 'lon'), may hold values from -6 to 6
- weights: bfloat16 [2, 512, 6144], P(None, 'lon'), may hold values from -4 to 4
- gains: float32 [2, 2, 512], replicated, may hold values from 0.1 to 1.9
Outputs:
- result: bfloat16 [2, 144, 768, 512], P(None, 'lat', 'lon')
All inputs are finite; a program needn't handle non-finite values.
Results may differ from a plain program's by a relative error of at most 0.012.
Values may be sent and summed in bfloat16 or wider, within the bound.
A program may use at most 128 MiB of HBM per device.

v0:
```python
import functools

import jax
import jax.numpy as jnp
import numpy as np
from jax import lax
from jax.experimental import pallas as pl
from jax.experimental.pallas import tpu as pltpu
from jax.sharding import PartitionSpec as P

F32, BF16 = jnp.float32, jnp.bfloat16
MESH = pl.DeviceIdType.MESH
NT = (((1,), (1,)), ((), ()))
TN = (((0,), (0,)), ((), ()))
NN = (((1,), (0,)), ((), ()))
T = 144
COUNT = 864
WIDTH = 512
STEPS = 6
SLAB = {(0, 0): 0, (1, 0): 32, (0, 1): 64, (1, 1): 96}
START = {(0, 0): 0, (1, 0): 36, (0, 1): 72, (1, 1): 108}
PLACE0 = {(0, 0): 0, (0, 1): 1, (1, 0): 2, (2, 0): 3, (1, 1): 4, (2, 1): 5}
PLACE1 = {(2, 0): 0, (2, 1): 1, (0, 1): 2, (1, 1): 3, (0, 0): 4, (1, 0): 5}


def place_matrices():
    into = np.zeros((288, 288), np.float32)
    out = np.zeros((288, 384), np.float32)
    shift = np.zeros((144, 192), np.float32)
    slabs = [(1, 1), (1, 0), (0, 1), (0, 0)]
    for j in range(2):
        for a in range(2):
            for b in range(2):
                for lev in range(2):
                    for r in range(3):
                        for c in range(6):
                            inner = lev * 18 + r * 6 + c
                            grid = lev * 144 + (a * 3 + r) * 24 + j * 12 + b * 6 + c
                            into[j * 144 + START[a, b] + inner, grid] = 1
                            source = (1 - a, 1 - b)
                            k = slabs.index(source) * 48 + START[source] - SLAB[source] + inner
                            out[grid, j * 192 + k] = 1
                            shift[START[a, b] + inner, k] = 1
    return into, shift, out


def device(x, y, z, c):
    return (lax.rem(x, 2) * 4 + y, (x // 2) * 16 + z * 2 + c)


def norm(v, gain):
    center = v - jnp.mean(v, axis=-1, keepdims=True)
    spread = jnp.mean(center * center, axis=-1, keepdims=True)
    return (center * lax.rsqrt(spread + 1e-5) * gain).astype(BF16)


def gelu(u):
    return 0.5 * u * (1.0 + lax.erf(u * np.float32(0.5**0.5)))


def kernel(
    x_ref, w_ref, g_ref, into_ref, shift_ref, out_ref, o_ref,
    W, X, N, QKV, ATT, R, H, Y, BIAS, HE, HS, HD, BW, BN, BD,
    send_z, send_x, send_y, send_c, recv_zx, recv_zy, recv_x, recv_y, recv_c, halo_send, halo_recv,
):
    lat, lon = lax.axis_index("lat"), lax.axis_index("lon")
    xlo, y = lat // 4, lax.rem(lat, 4)
    xhi, z, c = lon // 16, lax.rem(lon // 2, 8), lax.rem(lon, 2)
    x = xhi * 2 + xlo
    xn = 3 - x
    mine = xhi * 8 + z
    north = (lax.rem(lat + 7, 8), lon)
    south = (lax.rem(lat + 1, 8), lon)
    west = (lat, lax.rem(lon + 31, 32))
    east = (lat, lax.rem(lon + 1, 32))
    nw = (north[0], west[1])
    se = (south[0], east[1])
    sibling = device(x, y, z, 1 - c)
    ring_z = [device(x, y, lax.rem(z + d, 8), c) for d in range(1, 8)]
    cross_z = [device(xn, y, lax.rem(z + d, 8), c) for d in range(8)]
    peers_x = [device(lax.rem(x + d, 4), y, z, c) for d in range(1, 4)]
    peers_y = [device(x, lax.rem(y + d, 4), z, c) for d in range(1, 4)]
    halo = [west, north, nw, east, south, se]

    partners = [sibling] + ring_z + cross_z + peers_x + peers_y + halo
    barrier = pltpu.get_barrier_semaphore()
    for p in partners:
        pl.semaphore_signal(barrier, inc=1, device_id=p, device_id_type=MESH)

    xcols = pl.ds(pl.multiple_of(xlo * 512, 128), 512)
    ycols = pl.ds(pl.multiple_of(1024 + y * 256, 128), 256)
    for b in range(2):
        for f, from_x, from_y in (
            (3 * b, xlo * 512, 1024 + y * 256 + (y // 2) * 2048),
            (3 * b + 1, 1536 + xlo * 512, 2560 + y * 256),
            (3 * b + 2, 4096 + xlo * 512, 5120 + y * 256),
        ):
            W[f, mine, c, :, xcols] = w_ref[b, :, pl.ds(pl.multiple_of(from_x, 128), 512)]
            W[f, mine, c, :, ycols] = w_ref[b, :, pl.ds(pl.multiple_of(from_y, 128), 256)]
    pl.semaphore_wait(barrier, len(partners))

    xrows = pl.ds(xhi * 8, 8)

    def send(ref, s, r, to):
        pltpu.make_async_remote_copy(
            src_ref=ref, dst_ref=ref, send_sem=s, recv_sem=r, device_id=to, device_id_type=MESH
        ).start()

    def arrived(ref, s, r):
        pltpu.make_async_remote_copy(
            src_ref=ref, dst_ref=ref, send_sem=s, recv_sem=r, device_id=sibling, device_id_type=MESH
        ).wait_recv()

    def left(ref, s, r):
        pltpu.make_async_remote_copy(
            src_ref=ref, dst_ref=ref, send_sem=s, recv_sem=r, device_id=sibling, device_id_type=MESH
        ).wait_send()

    def s1(f):
        for to in ring_z:
            send(W.at[f, mine, c, :, xcols], send_z.at[f, 0], recv_zx.at[f], to)
        for to in ring_z + cross_z:
            send(W.at[f, mine, c, :, ycols], send_z.at[f, 1], recv_zy.at[f], to)

    def s2(f):
        arrived(W.at[f, 0:7, 0, :, 0:512], send_z.at[f, 0], recv_zx.at[f])
        for to in peers_x:
            send(W.at[f, xrows, c, :, xcols], send_x.at[f], recv_x.at[f], to)
        arrived(W.at[f, 0:15, 0, :, 0:256], send_z.at[f, 1], recv_zy.at[f])
        for to in peers_y:
            send(W.at[f, :, c, :, ycols], send_y.at[f], recv_y.at[f], to)

    def s3(f):
        arrived(W.at[f, 0:8, 0, :, 0:1536], send_x.at[f], recv_x.at[f])
        arrived(W.at[f, :, 0, :, 0:768], send_y.at[f], recv_y.at[f])
        send(W.at[f, :, c], send_c.at[f], recv_c.at[f], sibling)

    def s4(f):
        arrived(W.at[f, :, 0], send_c.at[f], recv_c.at[f])

    def drain(f):
        left(W.at[f, 0:7, 0, :, 0:512], send_z.at[f, 0], recv_zx.at[f])
        left(W.at[f, 0:15, 0, :, 0:256], send_z.at[f, 1], recv_zy.at[f])
        left(W.at[f, 0:8, 0, :, 0:1536], send_x.at[f], recv_x.at[f])
        left(W.at[f, :, 0, :, 0:768], send_y.at[f], recv_y.at[f])
        left(W.at[f, :, 0], send_c.at[f], recv_c.at[f])

    def weight(f, lo, n):
        return W[f, :, :, :, lo : lo + n].reshape(512, n)

    def rows_of(i, n):
        return pl.ds(pl.multiple_of(i * n, 16), n)

    def enter():
        for i in range(3):
            both = jnp.concatenate(
                [x_ref[144 * i : 144 * i + 144, :], x_ref[432 + 144 * i : 576 + 144 * i, :]], axis=0
            )
            tokens = lax.dot_general(into_ref[...], both, NN, preferred_element_type=F32)
            normed = norm(tokens, g_ref[0:1, :])
            for j in range(2):
                at = PLACE0[i, j] * T
                X[at : at + T, :] = tokens[j * T : j * T + T].astype(BF16)
                N[at : at + T, :] = normed[j * T : j * T + T]

    def project_in(f):
        def body(g, carry):
            rows = rows_of(g, 288)
            for k in range(3):
                part = jnp.dot(N[rows, :], weight(f, 512 * k, 512), preferred_element_type=F32)
                QKV[rows, 512 * k : 512 * k + 512] = part.astype(BF16)
            return carry

        lax.fori_loop(0, 3, body, 0)

    def attend(first, last, masked):
        low = lax.broadcasted_iota(jnp.int32, (T, 128), 1) < 64

        def body(w, carry):
            rows = rows_of(w, T)
            for p in range(4):
                q = QKV[rows, 128 * p : 128 * p + 128] * BF16(0.125)
                k = QKV[rows, 512 + 128 * p : 640 + 128 * p]
                v = QKV[rows, 1024 + 128 * p : 1152 + 128 * p]
                zero = jnp.zeros_like(q)
                pair = jnp.concatenate([jnp.where(low, q, zero), jnp.where(low, zero, q)], axis=0)
                s = lax.dot_general(k, pair, NT, preferred_element_type=F32)
                if masked:
                    s = s + BIAS[...]
                e = jnp.exp(s - jnp.max(s, axis=0, keepdims=True))
                probs = (e * (1.0 / jnp.sum(e, axis=0, keepdims=True))).astype(BF16)
                out = lax.dot_general(probs, v, TN, preferred_element_type=F32)
                ATT[rows, 128 * p : 128 * p + 128] = jnp.where(low, out[:T], out[T:]).astype(BF16)
            return carry

        lax.fori_loop(first, last, body, 0)

    def project_out(f, gain):
        def body(g, carry):
            rows = rows_of(g, 288)
            r = X[rows, :].astype(F32) + lax.dot_general(
                ATT[rows, :], weight(f, 1536, 512), NT, preferred_element_type=F32
            )
            R[rows, :] = r
            N[rows, :] = norm(r, g_ref[gain : gain + 1, :])
            return carry

        lax.fori_loop(0, 3, body, 0)

    def up(f):
        def body(g, carry):
            rows = rows_of(g, 288)
            for k in range(4):
                u = jnp.dot(N[rows, :], weight(f, 512 * k, 512), preferred_element_type=F32)
                H[rows, 512 * k : 512 * k + 512] = gelu(u).astype(BF16)
            return carry

        lax.fori_loop(0, 3, body, 0)

    def down(f, first, last):
        def body(g, carry):
            rows = rows_of(g, 288)
            total = R[rows, :]
            for k in range(4):
                total = total + lax.dot_general(
                    H[rows, 512 * k : 512 * k + 512], weight(f, 512 * k, 512), NT, preferred_element_type=F32
                )
            Y[rows, :] = total.astype(BF16)
            return carry

        lax.fori_loop(first, last, body, 0)

    def halo_pairs(forward):
        def y_rows(place, w, a, b):
            return Y.at[place[w] * T + a : place[w] * T + b, :]

        if forward:
            p = PLACE0
            return [
                (y_rows(p, (0, 0), 64, 112), HS.at[0, 64:112, :], north),
                (y_rows(p, (0, 1), 0, 112), HS.at[1, 0:112, :], north),
                (y_rows(p, (0, 0), 0, 48), HD.at[0:48, :], nw),
                (y_rows(p, (0, 0), 32, 80), HE.at[0, 32:80, :], west),
                (y_rows(p, (1, 0), 0, 80), HE.at[1, 0:80, :], west),
                (y_rows(p, (2, 0), 0, 80), HE.at[2, 0:80, :], west),
            ]
        p = PLACE1
        return [
            (y_rows(p, (2, 0), 32, 144), BN.at[0, 32:144, :], south),
            (y_rows(p, (2, 1), 32, 80), BN.at[1, 32:80, :], south),
            (y_rows(p, (2, 1), 96, 144), BD.at[96:144, :], se),
            (y_rows(p, (2, 1), 64, 112), BW.at[2, 64:112, :], east),
            (y_rows(p, (0, 1), 64, 144), BW.at[0, 64:144, :], east),
            (y_rows(p, (1, 1), 64, 144), BW.at[1, 64:144, :], east),
        ]

    def halo_copies(forward):
        base = 0 if forward else 6
        return [
            pltpu.make_async_remote_copy(
                src_ref=src, dst_ref=dst, send_sem=halo_send.at[base + i], recv_sem=halo_recv.at[base + i],
                device_id=to, device_id_type=MESH,
            )
            for i, (src, dst, to) in enumerate(halo_pairs(forward))
        ]

    def quarter(place, w, q):
        at = place[w] * T + SLAB[q]
        return Y[at : at + 48, :]

    def shift_windows(gain):
        def take(i, j, q):
            lo = SLAB[q]
            if i < 3 and j < 2:
                return quarter(PLACE0, (i, j), q)
            if i < 3:
                return HE[i, lo : lo + 48, :]
            if j < 2:
                return HS[j, lo : lo + 48, :]
            return HD[lo : lo + 48, :]

        for (i, j), at in PLACE1.items():
            parts = jnp.concatenate(
                [take(i, j, (1, 1)), take(i, j + 1, (1, 0)), take(i + 1, j, (0, 1)), take(i + 1, j + 1, (0, 0))],
                axis=0,
            )
            tokens = lax.dot_general(shift_ref[...], parts, NN, preferred_element_type=F32)
            X[at * T : at * T + T, :] = tokens.astype(BF16)
            N[at * T : at * T + T, :] = norm(tokens, g_ref[gain : gain + 1, :])

    def leave():
        def take(i, j, q):
            lo = SLAB[q]
            if i >= 0 and j >= 0:
                return quarter(PLACE1, (i, j), q)
            if i >= 0:
                return BW[i, lo : lo + 48, :]
            if j >= 0:
                return BN[j, lo : lo + 48, :]
            return BD[lo : lo + 48, :]

        for i in (2, 1, 0):
            parts = []
            for j in range(2):
                parts += [
                    take(i - 1, j - 1, (1, 1)), take(i - 1, j, (1, 0)), take(i, j - 1, (0, 1)), take(i, j, (0, 0)),
                ]
            tokens = lax.dot_general(
                out_ref[...], jnp.concatenate(parts, axis=0), NN, preferred_element_type=F32
            ).astype(BF16)
            o_ref[144 * i : 144 * i + 144, :] = tokens[:144]
            o_ref[432 + 144 * i : 576 + 144 * i, :] = tokens[144:]

    s1(0)
    s1(1)
    enter()
    key = lax.broadcasted_iota(jnp.int32, (T, 288), 0)
    query = lax.broadcasted_iota(jnp.int32, (T, 288), 1)
    query = jnp.where(query < T, query, query - T)

    def lower(t):
        return ((t >= 36) & (t < 72)) | (t >= 108)

    differ = jnp.where(lower(key), 1, 0) != jnp.where(lower(query), 1, 0)
    BIAS[...] = jnp.where(differ, jnp.where(lat == 7, jnp.float32(-1e30), jnp.float32(0)), jnp.float32(0))

    s2(0)
    s1(2)
    s2(1)
    s1(3)
    s3(0)
    s2(2)
    s4(0)
    project_in(0)
    s3(1)
    attend(0, 3, False)
    s1(4)
    s2(3)
    attend(3, 6, False)
    s3(2)
    project_out(0, 1)
    s4(1)
    s1(5)
    up(1)
    s2(4)
    s3(3)
    s4(2)
    there = halo_copies(True)
    down(2, 0, 1)
    for cp in there[:4]:
        cp.start()
    down(2, 1, 2)
    for cp in there[4:]:
        cp.start()
    down(2, 2, 3)
    s2(5)
    for cp in there:
        cp.wait_recv()
    shift_windows(2)
    s3(4)
    s4(3)
    project_in(3)
    attend(0, 2, True)
    s3(5)
    attend(2, 6, False)
    project_out(3, 3)
    s4(4)
    up(4)
    for cp in there:
        cp.wait_send()
    s4(5)
    back = halo_copies(False)
    down(5, 0, 1)
    for cp in back[:4]:
        cp.start()
    down(5, 1, 2)
    for cp in back[4:]:
        cp.start()
    down(5, 2, 3)
    for f in range(STEPS):
        drain(f)
    for cp in back:
        cp.wait_recv()
    leave()
    for cp in back:
        cp.wait_send()


def on_device(field, weights, gains):
    into, shift, out = (jnp.asarray(m, BF16) for m in place_matrices())
    vmem = pl.BlockSpec(memory_space=pltpu.VMEM)
    dma = pltpu.SemaphoreType.DMA
    result = pl.pallas_call(
        kernel,
        out_shape=jax.ShapeDtypeStruct((COUNT, WIDTH), BF16),
        in_specs=[vmem] * 6,
        out_specs=vmem,
        scratch_shapes=[
            pltpu.VMEM((STEPS, 16, 2, 16, 2048), BF16),
            pltpu.VMEM((COUNT, WIDTH), BF16),
            pltpu.VMEM((COUNT, WIDTH), BF16),
            pltpu.VMEM((COUNT, 3 * WIDTH), BF16),
            pltpu.VMEM((COUNT, WIDTH), BF16),
            pltpu.VMEM((COUNT, WIDTH), F32),
            pltpu.VMEM((COUNT, 4 * WIDTH), BF16),
            pltpu.VMEM((COUNT, WIDTH), BF16),
            pltpu.VMEM((T, 288), F32),
            pltpu.VMEM((3, T, WIDTH), BF16),
            pltpu.VMEM((2, T, WIDTH), BF16),
            pltpu.VMEM((T, WIDTH), BF16),
            pltpu.VMEM((3, T, WIDTH), BF16),
            pltpu.VMEM((2, T, WIDTH), BF16),
            pltpu.VMEM((T, WIDTH), BF16),
            dma((STEPS, 2)),
            dma((STEPS,)),
            dma((STEPS,)),
            dma((STEPS,)),
            dma((STEPS,)),
            dma((STEPS,)),
            dma((STEPS,)),
            dma((STEPS,)),
            dma((STEPS,)),
            dma((12,)),
            dma((12,)),
        ],
        compiler_params=pltpu.CompilerParams(
            collective_id=0, has_side_effects=True, vmem_limit_bytes=48 * 2**20
        ),
    )(field.reshape(COUNT, WIDTH), weights, gains.reshape(4, WIDTH), into, shift, out)
    return result.reshape(field.shape)


def solution(mesh):
    return jax.shard_map(
        on_device,
        mesh=mesh,
        in_specs=(P(None, "lat", "lon", None), P(None, "lon", None), P()),
        out_specs=P(None, "lat", "lon", None),
        check_vma=False,
    )
```

profile of v0, /device:TPU:1, one launch (start us, length us, event | category | flops | bytes accessed | tf_op | source)
XLA Modules:
  0.0 89.2 jit_solution(272146973050989902)
XLA Ops:
  0.0 0.7 reshape.10.g_ref
  0.7 0.0 copy-start
  0.7 1.2 %copy-done = bf16[2,18,24,512]{3,2,1,0:T(8,128)(2,1)S(1)} copy-done((bf16[2,18,24,512]{3,2,1,0:T(8,128)(2,1)S(1)}, bf16[2,18,24,512]{3,2,1,0:T(8,128)(2,1)}, u32[]{:S(2)}) %copy-start) | copy-done | bytes 884760
  1.9 0.0 copy-start.1
  1.9 1.0 %copy-done.1 = bf16[2,16,6144]{2,1,0:T(8,128)(2,1)S(1)} copy-done((bf16[2,16,6144]{2,1,0:T(8,128)(2,1)S(1)}, bf16[2,16,6144]{2,1,0:T(8,128)(2,1)}, u32[]{:S(2)}) %copy-start.1) | copy-done | bytes 393240
  2.9 0.0 copy-start.2
  2.9 0.9 %copy-done.2 = bf16[288,384]{1,0:T(8,128)(2,1)S(1)} copy-done((bf16[288,384]{1,0:T(8,128)(2,1)S(1)}, bf16[288,384]{1,0:T(8,128)(2,1)}, u32[]{:S(2)}) %copy-start.2) | copy-done | bytes 221208
  3.8 0.0 copy-start.3
  3.8 0.9 %copy-done.3 = bf16[288,288]{1,0:T(8,128)(2,1)S(1)} copy-done((bf16[288,288]{1,0:T(8,128)(2,1)S(1)}, bf16[288,288]{1,0:T(8,128)(2,1)}, u32[]{:S(2)}) %copy-start.3) | copy-done | bytes 165912
  4.7 0.0 copy-start.4
  4.8 0.9 copy-done.4
  5.6 82.6 %shard_map.64 = bf16[864,512]{1,0:T(8,128)(2,1)S(1)} custom-call(bf16[864,512]{1,0:T(8,128)(2,1)S(1)} %bitcast.3, bf16[2,16,6144]{2,1,0:T(8,128)(2,1)S(1)} %copy-done.1, f32[4,512]{1,0:T(4,128)S(1)} %reshape.10.g_ref, bf16[288,288]{1,0:T(8,128)(2,1)S(1)} %copy-done.3, bf16[144,192]{1,0:T(8,128)(2,1)S(1)} %copy-done.4, bf16[288,384]{1,0:T(8,128)(2,1)S(1)} %copy-done.2), custom_call_target="tpu_custom_call" | custom-call | tf_op jit(solution)/shard_map/pallas_call | solution.py:393
  88.3 0.9 %copy.8 = bf16[2,18,24,512]{3,2,1,0:T(8,128)(2,1)} copy(bf16[2,18,24,512]{3,2,1,0:T(8,128)(2,1)S(1)} %bitcast.2) | data formatting | bytes 1769472
Async XLA Ops:
  0.7 1.2 %copy-start = (bf16[2,18,24,512]{3,2,1,0:T(8,128)(2,1)S(1)}, bf16[2,18,24,512]{3,2,1,0:T(8,128)(2,1)}, u32[]{:S(2)}) copy-start(bf16[2,18,24,512]{3,2,1,0:T(8,128)(2,1)} %param.6) | copy-start | bytes 2654212
  1.9 1.0 %copy-start.1 = (bf16[2,16,6144]{2,1,0:T(8,128)(2,1)S(1)}, bf16[2,16,6144]{2,1,0:T(8,128)(2,1)}, u32[]{:S(2)}) copy-start(bf16[2,16,6144]{2,1,0:T(8,128)(2,1)} %w_ref.1) | copy-start | bytes 1179652
  2.9 0.9 %copy-start.2 = (bf16[288,384]{1,0:T(8,128)(2,1)S(1)}, bf16[288,384]{1,0:T(8,128)(2,1)}, u32[]{:S(2)}) copy-start(bf16[288,384]{1,0:T(8,128)(2,1)} %constant.8.clone.out_ref) | copy-start | bytes 663556
  3.8 0.9 %copy-start.3 = (bf16[288,288]{1,0:T(8,128)(2,1)S(1)}, bf16[288,288]{1,0:T(8,128)(2,1)}, u32[]{:S(2)}) copy-start(bf16[288,288]{1,0:T(8,128)(2,1)} %constant.6.clone.into_ref) | copy-start | bytes 497668
  4.7 0.9 copy-start.4
where the time goes:
time: 89.5 us; the launch traced here: 89.2 us
  Pallas kernels  82.6 us (92%)
  local copies, waits for them, and re-layouts  6.54 us (7%)
    pallas_call x1, Pallas kernels, on_device(): pl.pallas_call(kernel, out_shape=jax.ShapeDtypeStruct((COUNT, WIDTH), BF1...  82.6 us
    unnamed x11, local copies, waits for them, and re-layouts  5.83 us

commit v1 on v0

v1 whole, which is shorter than its diff:
```python
import functools

import jax
import jax.numpy as jnp
import numpy as np
from jax import lax
from jax.experimental import pallas as pl
from jax.experimental.pallas import tpu as pltpu
from jax.sharding import PartitionSpec as P

F32, BF16 = jnp.float32, jnp.bfloat16
MESH = pl.DeviceIdType.MESH
NT = (((1,), (1,)), ((), ()))
TN = (((0,), (0,)), ((), ()))
NN = (((1,), (0,)), ((), ()))
UNROLL = 2
T = 144
COUNT = 864
WIDTH = 512
PHASES = [
    (0, 0, 512, 1024, 1, 1),
    (0, 3072, 512, 512, 1, 1),
    (0, 1536, 1024, 512, 1, 1),
    (0, 4096, 1024, 1024, 1, 1),
    (1, 0, 512, 1024, 1, 1),
    (1, 1536, 1536, 1024, 1, 1),
    (1, 4096, 512, 512, 1, 1),
    (1, 5120, 512, 512, 1, 1),
]
STEPS = len(PHASES)
Z_TWO = [p[4] for p in PHASES]
XY_TWO = [p[5] for p in PHASES]
KINDS = ("zx", "zy", "fx", "fy", "x", "y", "gx", "gy", "cx", "cy")
SLAB = {(0, 0): 0, (1, 0): 32, (0, 1): 64, (1, 1): 96}
START = {(0, 0): 0, (1, 0): 36, (0, 1): 72, (1, 1): 108}
PLACE0 = {(0, 0): 0, (0, 1): 1, (1, 0): 2, (2, 0): 3, (1, 1): 4, (2, 1): 5}
PLACE1 = {(0, 1): 0, (1, 1): 1, (2, 0): 2, (2, 1): 3, (0, 0): 4, (1, 0): 5}


def place_matrices():
    into = np.zeros((288, 288), np.float32)
    shift = np.zeros((144, 192), np.float32)
    slabs = [(1, 1), (1, 0), (0, 1), (0, 0)]
    for j in range(2):
        for a in range(2):
            for b in range(2):
                for lev in range(2):
                    for r in range(3):
                        for c in range(6):
                            inner = lev * 18 + r * 6 + c
                            grid = lev * 144 + (a * 3 + r) * 24 + j * 12 + b * 6 + c
                            into[j * 144 + START[a, b] + inner, grid] = 1
                            source = (1 - a, 1 - b)
                            k = slabs.index(source) * 48 + START[source] - SLAB[source] + inner
                            shift[START[a, b] + inner, k] = 1
    return into, shift, into.T


def device(x, y, z, c):
    return (lax.rem(x, 2) * 4 + y, (x // 2) * 16 + z * 2 + c)


def norm(v, gain):
    center = v - jnp.mean(v, axis=-1, keepdims=True)
    spread = jnp.mean(center * center, axis=-1, keepdims=True)
    return (center * lax.rsqrt(spread + 1e-5) * gain).astype(BF16)


def gelu(u):
    return 0.5 * u * (1.0 + lax.erf(u * np.float32(0.5**0.5)))


def kernel(
    x_ref, w_ref, g_hbm, into_hbm, shift_hbm, out_hbm, o_ref,
    *refs
):
    WX, WY = refs[:STEPS], refs[STEPS : 2 * STEPS]
    (
    X, N, QKV, ATT, R, H, Y, BIAS, HE, HS, HD, BW, BN, BD,
    g_ref, into_ref, shift_ref, out_ref, local, send_sem, recv_sem, halo_send, halo_recv,
    ) = refs[2 * STEPS :]
    lat, lon = lax.axis_index("lat"), lax.axis_index("lon")
    xlo, y = lat // 4, lax.rem(lat, 4)
    xhi, z, c = lon // 16, lax.rem(lon // 2, 8), lax.rem(lon, 2)
    x = xhi * 2 + xlo
    xn = 3 - x
    north = (lax.rem(lat + 7, 8), lon)
    south = (lax.rem(lat + 1, 8), lon)
    west = (lat, lax.rem(lon + 31, 32))
    east = (lat, lax.rem(lon + 1, 32))
    nw = (north[0], west[1])
    se = (south[0], east[1])
    sibling = device(x, y, z, 1 - c)
    ring_z = [device(x, y, lax.rem(z + d, 8), c) for d in range(8)]
    cross_z = [device(xn, y, lax.rem(z + d, 8), c) for d in range(8)]
    peers_x = [device(lax.rem(x + d, 4), y, z, c) for d in range(4)]
    peers_y = [device(x, lax.rem(y + d, 4), z, c) for d in range(4)]
    halo = [west, north, nw, east, south, se]

    partners = [sibling] + ring_z[1:] + cross_z + peers_x[1:] + peers_y[1:] + halo
    barrier = pltpu.get_barrier_semaphore()
    for p in partners:
        pl.semaphore_signal(barrier, inc=1, device_id=p, device_id_type=MESH)

    def half_of(f, chip_x, x_hi, shards):
        return WX[f].at[lax.rem(chip_x, 2), c, x_hi, shards]

    def quarter_of(f, chip_y, x_hi, shards):
        return WY[f].at[chip_y, c, x_hi, shards]

    def own_rows(f):
        b, first, n, m = PHASES[f][:4]
        from_x = first + xlo * (n // 2)
        from_y = first + n + y * (m // 4)
        return [
            pltpu.make_async_copy(
                w_ref.at[b, :, pl.ds(pl.multiple_of(from_x, 128), n // 2)],
                half_of(f, x, xhi, z), local.at[2 * f],
            ),
            pltpu.make_async_copy(
                w_ref.at[b, :, pl.ds(pl.multiple_of(from_y, 128), m // 4)],
                quarter_of(f, y, xhi, z), local.at[2 * f + 1],
            ),
        ]

    own = [own_rows(f) for f in range(STEPS)]
    others = [
        pltpu.make_async_copy(src, dst, local.at[2 * STEPS + i])
        for i, (src, dst) in enumerate(
            [(x_ref, Y), (into_hbm, into_ref), (g_hbm, g_ref), (shift_hbm, shift_ref), (out_hbm, out_ref)]
        )
    ]
    for cp in own[0] + others[:3] + sum(own[1:], []) + others[3:]:
        cp.start()
    for cp in own[0]:
        cp.wait()
    pl.semaphore_wait(barrier, len(partners))

    def copy(f, kind, ref, to):
        k = KINDS.index(kind)
        return pltpu.make_async_remote_copy(
            src_ref=ref, dst_ref=ref, send_sem=send_sem.at[f, k], recv_sem=recv_sem.at[f, k],
            device_id=to, device_id_type=MESH,
        )

    def total(f, kind):
        far, two = 1 - Z_TWO[f], XY_TWO[f]
        h, q = WX[f], WY[f]
        return {
            "zx": h.at[0, 0, 0, 0 : 7 if far else 4],
            "zy": q.at[0:3, 0, 0, 0 : 5 if far else 3],
            "fx": h.at[0, 0, 0, 0:3],
            "fy": q.at[0, 0, :, 0:3],
            "x": h.at[0, 0] if two else h.at[0, :, :, 0:6],
            "y": q.at[0 : 2 if two else 3, 0],
            "gx": h.at[0, 0, 0],
            "gy": q.at[0, 0],
            "cx": h.at[:, 0],
            "cy": q.at[:, 0],
        }[kind]

    def arrived(f, *kinds):
        for kind in kinds:
            copy(f, kind, total(f, kind), sibling).wait_recv()

    def z_near(f):
        if f:
            for cp in own[f]:
                cp.wait()
        ways = (1, 7, 2, 6) if Z_TWO[f] else (1, 7, 2, 6, 3, 5, 4)
        cross = (0, 1, 7, 2, 6) if Z_TWO[f] else (0, 1, 7, 2, 6, 3, 5, 4)
        mine_x = half_of(f, x, xhi, z)
        mine_y = quarter_of(f, y, xhi, z)
        for d in ways:
            copy(f, "zx", mine_x, ring_z[d]).start()
        for d in ways:
            copy(f, "zy", mine_y, ring_z[d]).start()
        for d in cross:
            copy(f, "zy", mine_y, cross_z[d]).start()

    def z_far(f):
        arrived(f, "zx", "zy")
        below, above = lax.rem(z + 6, 8), lax.rem(z + 2, 8)
        for shard, d in ((below, 1), (above, 7), (below, 2)):
            copy(f, "fx", half_of(f, x, xhi, shard), ring_z[d]).start()
        for shard, d in ((below, 1), (above, 7), (above, 6)):
            copy(f, "fy", quarter_of(f, y, slice(None), shard), ring_z[d]).start()

    def xy_near(f):
        arrived(f, *(("fx", "fy") if Z_TWO[f] else ("zx", "zy")))
        for d in (1, 3) if XY_TWO[f] else (1, 3, 2):
            copy(f, "x", half_of(f, x, xhi, slice(None)), peers_x[d]).start()
        for d in (1, 3) if XY_TWO[f] else (1, 3, 2):
            copy(f, "y", quarter_of(f, y, slice(None), slice(None)), peers_y[d]).start()

    def xy_far(f):
        arrived(f, "x", "y")
        below, above = lax.rem(x + 3, 4), lax.rem(x + 1, 4)
        copy(f, "gx", half_of(f, below, below // 2, slice(0, 4)), peers_x[1]).start()
        copy(f, "gx", half_of(f, above, above // 2, slice(4, 8)), peers_x[3]).start()
        below, above = lax.rem(y + 3, 4), lax.rem(y + 1, 4)
        copy(f, "gy", quarter_of(f, below, 0, slice(None)), peers_y[1]).start()
        copy(f, "gy", quarter_of(f, above, 1, slice(None)), peers_y[3]).start()

    def share(f):
        arrived(f, *(("gx", "gy") if XY_TWO[f] else ("x", "y")))
        copy(f, "cx", WX[f].at[:, c], sibling).start()
        copy(f, "cy", WY[f].at[:, c], sibling).start()

    def ready(f):
        arrived(f, "cx", "cy")

    def drain(f):
        kinds = ("zx", "zy", "x", "y", "cx", "cy") + ("fx", "fy") * Z_TWO[f] + ("gx", "gy") * XY_TWO[f]
        for kind in kinds:
            copy(f, kind, total(f, kind), sibling).wait_send()

    def weight(block, lo, n):
        f = [
            i for i, p in enumerate(PHASES) if p[0] == block and p[1] <= lo and lo + n <= p[1] + p[2] + p[3]
        ][0]
        lo -= PHASES[f][1]
        parts = []
        while n:
            if lo < PHASES[f][2]:
                ref, size, at = WX[f], PHASES[f][2] // 2, lo
            else:
                ref, size, at = WY[f], PHASES[f][3] // 4, lo - PHASES[f][2]
            begin = at % size
            take = min(n, size - begin)
            cores = [ref[at // size, k, :, :, :, begin : begin + take] for k in range(2)]
            parts.append(jnp.stack(cores, axis=2).reshape(512, take))
            lo, n = lo + take, n - take
        return parts[0] if len(parts) == 1 else jnp.concatenate(parts, axis=1)

    def loop(n, body, hooks, first=0):
        def step(g, carry):
            for i, hook in hooks.items():
                pl.when(g == i)(hook)
            body(g)
            return carry

        lax.fori_loop(first, n, step, 0)

    def rows_of(i, n):
        return pl.ds(pl.multiple_of(i * n, 16), n)

    def enter():
        for i in range(3):
            both = jnp.concatenate(
                [Y[144 * i : 144 * i + 144, :], Y[432 + 144 * i : 576 + 144 * i, :]], axis=0
            )
            tokens = lax.dot_general(into_ref[...], both, NN, preferred_element_type=F32)
            normed = norm(tokens, g_ref[0, 0:1, :])
            for j in range(2):
                at = PLACE0[i, j] * T
                X[at : at + T, :] = tokens[j * T : j * T + T].astype(BF16)
                N[at : at + T, :] = normed[j * T : j * T + T]

    def project_in(block, k):
        for n in range(512 * k, 512 * k + 512, 256):
            QKV[:, n : n + 256] = jnp.dot(N[...], weight(block, n, 256), preferred_element_type=F32).astype(BF16)

    def attend(block, hooks):
        low = lax.broadcasted_iota(jnp.int32, (T, 128), 1) < 64

        def body(g):
            for w in range(3):
                for p in range(4):
                    rows = rows_of(3 * g + w, T)
                    at = 128 * p
                    q = QKV[rows, at : at + 128] * BF16(0.125)
                    k = QKV[rows, at + 512 : at + 640]
                    v = QKV[rows, at + 1024 : at + 1152]
                    zero = jnp.zeros_like(q)
                    pair = jnp.concatenate([jnp.where(low, q, zero), jnp.where(low, zero, q)], axis=0)
                    s = lax.dot_general(k, pair, NT, preferred_element_type=F32)
                    if block and w != 1:
                        s = s + BIAS[g if w == 0 else 1 - g]
                    e = jnp.exp(s - jnp.max(s, axis=0, keepdims=True))
                    probs = (e * (1.0 / jnp.sum(e, axis=0, keepdims=True))).astype(BF16)
                    out = lax.dot_general(probs, v, TN, preferred_element_type=F32)
                    ATT[rows, at : at + 128] = jnp.where(low, out[:T], out[T:]).astype(BF16)

        loop(2, body, hooks)

    def project_out(block, hooks):
        def body(g):
            rows = rows_of(g, 432)
            base, attended = (Y[rows, :], QKV[rows, 0:512]) if block else (X[rows, :], ATT[rows, :])
            r = base.astype(F32) + lax.dot_general(
                attended, weight(block, 3584, 512), NT, preferred_element_type=F32
            )
            R[rows, :] = r
            N[rows, :] = norm(r, g_ref[block, 1:2, :])

        loop(2, body, hooks)

    def up(block, k):
        for n in range(512 * k, 512 * k + 512, 256):
            u = jnp.dot(N[...], weight(block, 1536 + n, 256), preferred_element_type=F32)
            H[:, n : n + 256] = gelu(u).astype(BF16)

    def down(block, k, hooks):
        def body(g):
            rows = rows_of(g, 288)
            acc = R[rows, :] + lax.dot_general(
                H[rows, 1024 * k : 1024 * k + 1024], weight(block, 4096 + 1024 * k, 1024), NT,
                preferred_element_type=F32,
            )
            if k and block:
                X[rows, :] = acc.astype(BF16)
            elif k:
                Y[rows, :] = acc.astype(BF16)
            else:
                R[rows, :] = acc

        loop(3, body, hooks)

    def halo_pairs(forward):
        def y_rows(place, w, a, b):
            return (Y if forward else ATT).at[place[w] * T + a : place[w] * T + b, :]

        if forward:
            p = PLACE0
            return [
                (y_rows(p, (0, 0), 64, 112), HS.at[0, 64:112, :], north),
                (y_rows(p, (0, 1), 0, 112), HS.at[1, 0:112, :], north),
                (y_rows(p, (0, 0), 0, 48), HD.at[0:48, :], nw),
                (y_rows(p, (0, 0), 32, 80), HE.at[0, 32:80, :], west),
                (y_rows(p, (1, 0), 0, 80), HE.at[1, 0:80, :], west),
                (y_rows(p, (2, 0), 0, 80), HE.at[2, 0:80, :], west),
            ]
        p = PLACE1
        return [
            (y_rows(p, (0, 1), 64, 144), BW.at[0, 64:144, :], east),
            (y_rows(p, (1, 1), 64, 144), BW.at[1, 64:144, :], east),
            (y_rows(p, (2, 1), 64, 112), BW.at[2, 64:112, :], east),
            (y_rows(p, (2, 0), 32, 144), BN.at[0, 32:144, :], south),
            (y_rows(p, (2, 1), 32, 80), BN.at[1, 32:80, :], south),
            (y_rows(p, (2, 1), 96, 144), BD.at[96:144, :], se),
        ]

    def halo_copies(forward):
        base = 0 if forward else 6
        return [
            pltpu.make_async_remote_copy(
                src_ref=src, dst_ref=dst, send_sem=halo_send.at[base + i], recv_sem=halo_recv.at[base + i],
                device_id=to, device_id_type=MESH,
            )
            for i, (src, dst, to) in enumerate(halo_pairs(forward))
        ]

    def quarter(ref, place, w, q):
        at = place[w] * T + SLAB[q]
        return ref[at : at + 48, :]

    def shift_windows():
        def take(i, j, q):
            lo = SLAB[q]
            if i < 3 and j < 2:
                return quarter(Y, PLACE0, (i, j), q)
            if i < 3:
                return HE[i, lo : lo + 48, :]
            if j < 2:
                return HS[j, lo : lo + 48, :]
            return HD[lo : lo + 48, :]

        for (i, j), at in PLACE1.items():
            parts = jnp.concatenate(
                [take(i, j, (1, 1)), take(i, j + 1, (1, 0)), take(i + 1, j, (0, 1)), take(i + 1, j + 1, (0, 0))],
                axis=0,
            )
            tokens = lax.dot_general(shift_ref[...], parts, NN, preferred_element_type=F32)
            N[at * T : at * T + T, :] = norm(tokens, g_ref[1, 0:1, :])

    def unshift():
        def take(i, j, q):
            lo = SLAB[q]
            if i >= 0 and j >= 0:
                return quarter(ATT, PLACE1, (i, j), q)
            if i >= 0:
                return BW[i, lo : lo + 48, :]
            if j >= 0:
                return BN[j, lo : lo + 48, :]
            return BD[lo : lo + 48, :]

        for (i, j), at in PLACE0.items():
            parts = [take(i - 1, j - 1, (1, 1)), take(i - 1, j, (1, 0)), take(i, j - 1, (0, 1)), take(i, j, (0, 0))]
            rows = lax.dot_general(
                shift_ref[...], jnp.concatenate(parts, axis=0), NN, preferred_element_type=F32
            )
            QKV[at * T : at * T + T, 0:512] = rows.astype(BF16)

    def leave():
        for i in range(3):
            pair = [X[PLACE0[i, j] * T : PLACE0[i, j] * T + T, :] for j in range(2)]
            tokens = lax.dot_general(
                out_ref[...], jnp.concatenate(pair, axis=0), NN, preferred_element_type=F32
            ).astype(BF16)
            o_ref[144 * i : 144 * i + 144, :] = tokens[:144]
            o_ref[432 + 144 * i : 576 + 144 * i, :] = tokens[144:]

    z_near(0)
    z_near(1)
    z_near(2)
    for cp in others:
        cp.wait()
    enter()
    z_near(3)
    key = lax.broadcasted_iota(jnp.int32, (T, 288), 0)
    query = lax.broadcasted_iota(jnp.int32, (T, 288), 1)
    query = jnp.where(query < T, query, query - T)

    def lower(t):
        return ((t >= 36) & (t < 72)) | (t >= 108)

    differ = jnp.where(lower(key), 1, 0) != jnp.where(lower(query), 1, 0)
    BIAS[0] = jnp.zeros((T, 288), F32)
    BIAS[1] = jnp.where(differ, jnp.where(lat == 7, jnp.float32(-1e30), jnp.float32(0)), jnp.float32(0))
    z_far(0)
    z_far(1)
    z_near(4)
    z_far(2)
    z_far(3)
    xy_near(0)
    z_near(5)
    xy_near(1)
    z_far(4)
    xy_near(2)
    z_near(6)
    xy_far(0)
    xy_near(3)
    z_near(7)
    xy_far(1)
    z_far(5)
    xy_far(2)
    xy_near(4)
    share(0)
    z_far(6)
    z_far(7)
    ready(0)
    project_in(0, 0)
    project_in(0, 1)
    xy_far(3)
    project_in(0, 2)
    share(1)
    xy_near(5)
    xy_near(6)

    def hook0():
        ready(1)
        share(2)
        xy_near(7)

    attend(0, {1: hook0})
    xy_far(4)

    def hook1():
        ready(2)
        share(3)

    project_out(0, {1: hook1})
    up(0, 3)
    up(0, 0)
    up(0, 1)
    up(0, 2)
    ready(3)

    def hook2():
        xy_far(5)

    down(0, 0, {2: hook2})
    there = halo_copies(True)

    def hook3():
        for cp in there[:4]:
            cp.start()
        xy_far(6)


    def hook4():
        for cp in there[4:]:
            cp.start()

    down(0, 1, {1: hook3, 2: hook4})
    xy_far(7)
    share(4)
    for cp in there:
        cp.wait_recv()
    shift_windows()
    share(5)
    ready(4)
    project_in(1, 0)
    share(6)
    project_in(1, 1)
    project_in(1, 2)
    share(7)
    back = halo_copies(False)

    def hook5():
        for k in (3, 0, 1):
            back[k].start()
        ready(5)

    attend(1, {1: hook5})
    for k in (4, 5, 2):
        back[k].start()
    ready(6)
    ready(7)
    for cp in back:
        cp.wait_recv()
    unshift()
    project_out(1, {})
    up(1, 3)
    up(1, 0)
    up(1, 1)
    up(1, 2)
    down(1, 0, {})
    down(1, 1, {})
    leave()
    for f in range(STEPS):
        drain(f)
    for cp in there + back:
        cp.wait_send()


def on_device(field, weights, gains):
    into, shift, out = (jnp.asarray(m, BF16) for m in place_matrices())
    dma = pltpu.SemaphoreType.DMA
    tokens = [pltpu.VMEM((COUNT, n), t) for n, t in (
        (512, BF16), (512, BF16), (1536, BF16), (512, BF16), (512, F32), (2048, BF16), (512, BF16)
    )]
    halos = [pltpu.VMEM(n + (T, WIDTH), BF16) for n in ((3,), (2,), (), (3,), (2,), ())]
    result = pl.pallas_call(
        kernel,
        out_shape=jax.ShapeDtypeStruct((COUNT, WIDTH), BF16),
        in_specs=[pl.BlockSpec(memory_space=pl.ANY)] * 6,
        out_specs=pl.BlockSpec(memory_space=pltpu.VMEM),
        scratch_shapes=[pltpu.VMEM((2, 2, 2, 8, 16, p[2] // 2), BF16) for p in PHASES]
        + [pltpu.VMEM((4, 2, 2, 8, 16, p[3] // 4), BF16) for p in PHASES]
        + tokens
        + [pltpu.VMEM((2, T, 288), F32)]
        + halos
        + [
            pltpu.VMEM((2, 2, WIDTH), F32),
            pltpu.VMEM((288, 288), BF16),
            pltpu.VMEM((T, 192), BF16),
            pltpu.VMEM((288, 288), BF16),
            dma((2 * STEPS + 5,)),
            dma((STEPS, len(KINDS))),
            dma((STEPS, len(KINDS))),
            dma((12,)),
            dma((12,)),
        ],
        compiler_params=pltpu.CompilerParams(
            collective_id=0, has_side_effects=True, vmem_limit_bytes=56 * 2**20
        ),
    )(field.reshape(COUNT, WIDTH), weights, gains, into, shift, out)
    return result.reshape(field.shape)


def solution(mesh):
    return jax.shard_map(
        on_device,
        mesh=mesh,
        in_specs=(P(None, "lat", "lon", None), P(None, "lon", None), P()),
        out_specs=P(None, "lat", "lon", None),
        check_vma=False,
    )
```

time: 89.5 us -> 80.6 us (0.901)
  local copies, waits for them, and re-layouts: 6.54 us -> 2.15 us
  Pallas kernels: 82.6 us -> 78.3 us
    pallas_call x1, Pallas kernels: 82.6 us -> 78.3 us  [on_device(): pl.pallas_call(kernel, out_shape=jax.ShapeDtypeStruct((COUNT, WIDTH), BF1...]
    unnamed x11 -> x1, local copies, waits for them, and re-layouts: 5.83 us -> 2.15 us
where the time goes in v1:
time: 80.6 us; the launch traced here: 80.5 us
  Pallas kernels  78.3 us (97%)
  local copies, waits for them, and re-layouts  2.15 us (3%)
    pallas_call x1, Pallas kernels, on_device(): pl.pallas_call(kernel, out_shape=jax.ShapeDtypeStruct((COUNT, WIDTH), BF1...  78.3 us
    unnamed x1, local copies, waits for them, and re-layouts  2.15 us

profile of v1, /device:TPU:1, one launch (start us, length us, event | category | flops | bytes accessed | tf_op | source)
XLA Modules:
  0.0 80.5 jit_solution(5718753862508139656)
XLA Ops:
  0.0 78.3 %shard_map.64 = bf16[864,512]{1,0:T(8,128)(2,1)} custom-call(bf16[864,512]{1,0:T(8,128)(2,1)} %bitcast.3, bf16[2,16,6144]{2,1,0:T(8,128)(2,1)} %w_ref.1, f32[2,2,512]{2,1,0:T(2,128)} %g_hbm.1, bf16[288,288]{1,0:T(8,128)(2,1)} %constant.6.clone.into_hbm, bf16[144,192]{1,0:T(8,128)(2,1)} %constant.7.clone.shift_hbm, bf16[288,288]{1,0:T(8,128)(2,1)} %constant.8.clone.out_hbm), custom_call_target="tpu_custom_call" | custom-call | tf_op jit(solution)/shard_map/pallas_call | solution.py:535
  78.3 2.1 %copy.8 = bf16[2,18,24,512]{3,2,1,0:T(8,128)(2,1)} copy(bf16[2,18,24,512]{3,2,1,0:T(8,128)(2,1)} %bitcast.2) | data formatting | bytes 1769472
